TPU v7x, 128 devices: a whole 4x4x4 slice. The times are simulated.
128 devices in a mesh: row: 4 (over x_lo, core), col: 32 (over y, z, x_hi).
Axes of the slice: x: 4 (x_hi: 2, x_lo: 2; x = x_hi * 2 + x_lo), y: 4, z: 4, core: 2. Of those that a mesh axis runs over, the one named last changes fastest.
Arguments:
- x2_rows: bfloat16 [8192, 2048], P(('row', 'col')), may hold values from -0.21875 to 0.21875
- x_panels: bfloat16 [4, 512, 45056], P('row', None, 'col'), may hold values from -6 to 6
- panel_mask: int32 [4, 4, 352], P('row', None, 'col'), may hold values 0 or 1
- owners: int32 [4], replicated, may hold values from 0 to 3, each once
- x2_tile: bfloat16 [8192, 45056], P('row', 'col'), may hold values from -3 to 3
- block_ids: int32 [6144], P(('row', 'col')), may hold values from 0 to 175, as said below
- dest: int32 [6144, 1], P(('row', 'col')), may hold values from 0 to 31; in each aligned block of 48 rows (0 to 47, 48 to 95, ...) at most 2 rows name the same one
- counts: int32 [128], P(('row', 'col')), may hold values from 24 to 48
Outputs:
- purified: bfloat16 [8192, 128, 128], P(('row', 'col'))
Inputs may be any that keep to these rules, and one draw needn't show every extreme that they name: `block_ids`: no two of one device's 48 entries are equal. `dest`: among one device's 48 entries no owner is named more than 2 times. `owners`: each slot is named once.
All inputs are finite; a program needn't handle non-finite values. No bound on the sum of `panel_mask` on one device may be relied on, other than what follows from the above.
Results may differ from a plain program's by a relative error of at most 0.001.
Values may be sent and summed in bfloat16 or wider, within the bound.
A program may use at most 128 MiB of HBM per device.

v0:
```python
import jax
import jax.numpy as jnp
from jax import lax
from jax.sharding import PartitionSpec as P

BS = 128
CB_DEV = 11
PB = 4


def broadcast(x, axis, root):
    mine = lax.axis_index(axis) == root
    return lax.psum(jnp.where(mine, x, jnp.zeros_like(x)), axis)


def select_blocks(full_tile, listed):
    row_count = full_tile.shape[0] // BS
    shaped = full_tile.reshape(row_count, BS, CB_DEV, BS).transpose(0, 2, 1, 3)
    return jnp.take(shaped.reshape(row_count * CB_DEV, BS, BS), listed, axis=0)


def shards(x2_rows, x_panels, panel_mask, owners, x2_tile, block_ids, dest, counts):
    panel_count = lax.axis_size("row")
    col_count = lax.axis_size("col")
    panel_depth = PB * BS
    cell_mask = jnp.broadcast_to(panel_mask[:, :, None, :, None], (1, PB, BS, CB_DEV, BS))
    own_panel = x_panels * cell_mask.reshape(1, panel_depth, CB_DEV * BS).astype(jnp.bfloat16)
    panels = [broadcast(own_panel, "row", owners[panel])[0] for panel in range(panel_count)]
    whole_rows = lax.all_gather(x2_rows, "col", axis=0, tiled=True)
    cube_term = select_blocks(
        jnp.dot(whole_rows, jnp.concatenate(panels, axis=0), preferred_element_type=jnp.float32),
        block_ids,
    )
    square_term = select_blocks(x2_tile, block_ids).astype(jnp.float32)
    entry_count = block_ids.shape[0]
    alive_mask = jnp.arange(entry_count, dtype=jnp.int32) < counts[0]
    blocks = jnp.where(
        alive_mask[:, None, None], 3.0 * square_term - 2.0 * cube_term, jnp.zeros_like(cube_term)
    ).astype(jnp.bfloat16)
    capacity = max(2, (entry_count + col_count - 1) // col_count)
    owner_col = dest[:, 0]
    one_hot = (owner_col[:, None] == jnp.arange(col_count, dtype=jnp.int32)[None, :]).astype(
        jnp.int32
    )
    slot_rank = jnp.sum((jnp.cumsum(one_hot, axis=0) - one_hot) * one_hot, axis=1)
    outgoing = (
        jnp.zeros((col_count * capacity, BS, BS), jnp.bfloat16)
        .at[owner_col * capacity + slot_rank]
        .set(blocks)
    )
    incoming = lax.all_to_all(
        outgoing.reshape(col_count, capacity, BS, BS),
        "col",
        split_axis=0,
        concat_axis=0,
        tiled=True,
    )
    return incoming.reshape(col_count * capacity, BS, BS)


def solution(mesh):
    return jax.shard_map(
        shards,
        mesh=mesh,
        in_specs=(
            P(("row", "col"), None),
            P("row", None, "col"),
            P("row", None, "col"),
            P(),
            P("row", "col"),
            P(("row", "col")),
            P(("row", "col"), None),
            P(("row", "col")),
        ),
        out_specs=P(("row", "col"), None, None),
        check_vma=False,
    )
```

profile of v0, /device:TPU:0, one launch (start us, length us, event | category | flops | bytes accessed | tf_op | source)
XLA Modules:
  0.0 275.6 jit_solution(2833050154562239565)
XLA Ops:
  7.4 0.0 all-reduce.3.cloned.1.call-start
  7.4 1.4 fusion.14
  8.8 0.7 convert_bitcast_fusion
  9.5 0.1 copy.11
  9.6 0.5 broadcast_in_dim.48
  10.0 0.6 convert_element_type.31
  10.6 1.7 copy.12
  14.7 1.3 select_bitcast_fusion.3
  16.1 2.1 select_bitcast_fusion.2
  18.2 0.0 all-reduce.3.cloned.1.call-update
  18.2 0.0 all-gather.2.cloned.1.call-start
  18.3 0.5 all-gather.2.cloned.1.call-update
  18.8 8.2 %copy.9 = bf16[2048,1408]{0,1:T(8,128)(2,1)} copy(bf16[2048,1408]{1,0:T(8,128)(2,1)} %param.12) | data formatting | bytes 11534336 | tf_op args[4]
  27.0 7.4 %copy.14 = bf16[176,8,16,128]{3,2,1,0:T(8,128)(2,1)} copy(bf16[176,8,16,128]{3,1,2,0:T(8,128)(2,1)} %bitcast.48) | data formatting | bytes 11534336
  34.5 0.0 copy-start.1
  34.5 8.9 %copy.10 = bf16[16,11,128,128]{3,2,1,0:T(8,128)(2,1)} copy(bf16[16,11,128,128]{2,0,3,1:T(8,128)(2,1)} %bitcast.47) | data formatting | bytes 11534336 | tf_op jit(solution)/shard_map/transpose | solution.py:18
  43.4 0.0 copy-start
  44.0 0.0 copy-done.1
  44.1 4.6 %gather_fusion = bf16[48,128,128]{2,1,0:T(8,128)(2,1)} fusion(bf16[176,128,128]{2,1,0:T(8,128)(2,1)} %bitcast.51, s32[1024]{0:T(1024)S(1)} %pad_clamp_fusion), kind=kCustom, calls=%fused_computation | custom fusion | bytes 3145920 | tf_op jit(solution)/shard_map/jit(_take)/gather | solution.py:19
  48.7 0.0 copy-done
  48.7 0.1 fusion.11
  48.8 0.1 reduce_window_sum.11
  48.8 0.2 select_reduce_fusion
  49.0 121.2 %all-reduce.3.cloned.1.call-done = (bf16[512,1408]{0,1:T(8,128)(2,1)}, bf16[512,1408]{0,1:T(8,128)(2,1)}, bf16[512,1408]{0,1:T(8,128)(2,1)}, bf16[512,1408]{0,1:T(8,128)(2,1)}) async-done(((bf16[512,1408]{0,1:T(8,128)(2,1)}, bf16[512,1408]{0,1:T(8,128)(2,1)}, bf16[512,1408]{0,1:T(8,128)(2,1)}, bf16[512,1408]{0,1:T(8,128)(2,1)}), (bf16[512,1408]{0,1:T(8,128)(2,1)}, bf16[512,1408]{0,1:T(8,128)(2,1)}, ...) | async-done | bytes 5767184 | tf_op jit(solution)/shard_map/psum | solution.py:13
  170.2 0.0 all-gather.2.cloned.1.call-done
  170.2 18.6 %fusion.8 = f32[176,8,16,128]{3,1,2,0:T(8,128)} fusion(bf16[2048,2048]{1,0:T(8,128)(2,1)} %all-gather.2.cloned.1.call-done, bf16[512,1408]{0,1:T(8,128)(2,1)} %get-tuple-element.5, bf16[512,1408]{0,1:T(8,128)(2,1)} %get-tuple-element.6, bf16[512,1408]{0,1:T(8,128)(2,1)} %get-tuple-element.7, bf16[512,1408]{0,1:T(8,128)(2,1)} %get-tuple-element.8), kind=kOutput, calls=%fused_computation.11 | convolution fusion | flops 11834228736 | bytes 25690112 | tf_op jit(solution)/shard_map/dot_general | solution.py:31
  188.9 11.3 %copy.15 = f32[176,8,16,128]{3,2,1,0:T(8,128)} copy(f32[176,8,16,128]{3,1,2,0:T(8,128)} %fusion.8) | data formatting | bytes 23068672
  200.1 12.3 %copy.13 = f32[16,128,11,128]{3,1,2,0:T(8,128)} copy(f32[16,128,11,128]{1,0,3,2:T(8,128)} %bitcast.46) | data formatting | bytes 23068672 | tf_op jit(solution)/shard_map/reshape | solution.py:18
  212.5 5.0 %gather_fusion.1 = f32[48,128,128]{2,1,0:T(8,128)S(1)} fusion(f32[176,128,128]{2,1,0:T(8,128)} %bitcast.49, s32[1024]{0:T(1024)S(1)} %pad_clamp_fusion), kind=kCustom, calls=%fused_computation.1 | custom fusion | bytes 6291648 | tf_op jit(solution)/shard_map/jit(_take)/gather | solution.py:19
  217.5 3.4 %select_convert_fusion = bf16[48,128,128]{2,1,0:T(8,128)(2,1)} fusion(f32[48,128,128]{2,1,0:T(8,128)S(1)} %gather_fusion.1, bf16[48,128,128]{2,1,0:T(8,128)(2,1)} %gather_fusion, pred[48]{0:T(512)(128)(4,1)S(1)} %get-tuple-element.18, pred[48]{0:T(512)(128)(4,1)S(1)} %get-tuple-element.19), kind=kLoop, calls=%fused_computation.12 | loop fusion | flops 6291456 | bytes 6291552 | tf_op jit(solution)/shard_map/convert_element_type | solution.py:39
  221.0 0.5 broadcast_in_dim.43
  221.5 5.1 %scatter_fusion = bf16[64,128,128]{2,1,0:T(8,128)(2,1)S(1)} fusion(bf16[64,128,128]{2,1,0:T(8,128)(2,1)S(1)} %broadcast_in_dim.43, s32[48]{0:T(128)S(1)} %fusion.12, bf16[48,128,128]{2,1,0:T(8,128)(2,1)} %select_convert_fusion), kind=kCustom, calls=%fused_computation.2 | custom fusion | bytes 4718784 | tf_op jit(solution)/shard_map/scatter | solution.py:49
  226.6 40.3 %all_to_all.5 = bf16[32,2,128,128]{3,2,1,0:T(8,128)(2,1)S(1)} all-to-all(bf16[32,2,128,128]{3,2,1,0:T(8,128)(2,1)S(1)} %bitcast.50), channel_id=1, replica_groups=mesh['row'=4,'col'=32] {'col'}, dimensions={0} | all-to-all | bytes 4194304 | tf_op jit(solution)/shard_map/all_to_all | solution.py:51
  266.8 1.3 copy.23
  (4 shorter events, 0.0 us)
Async XLA Ops:
  7.4 162.9 %all-reduce.3.cloned.1.call-start = ((), (), s32[]{:S(2)}) async-start(), calls=%async_computation.2 | async-start | bytes 11534336 | tf_op jit(solution)/shard_map/psum | solution.py:13
  18.2 152.0 %all-gather.2.cloned.1.call-start = ((), (), s32[]{:S(2)}) async-start(), calls=%async_computation.1 | async-start | bytes 8650752 | tf_op jit(solution)/shard_map/all_gather | solution.py:29
  34.5 9.6 %copy-start.1 = (s32[48]{0:T(128)S(1)}, s32[48]{0:T(128)}, u32[]{:S(2)}) copy-start(s32[48]{0:T(128)} %param.13) | copy-start | bytes 580
  43.4 5.3 %copy-start = (s32[48,1]{0,1:T(1,128)S(1)}, s32[48,1]{0,1:T(1,128)}, u32[]{:S(2)}) copy-start(s32[48,1]{0,1:T(1,128)} %param.14) | copy-start | bytes 580
Sparse Core Ops, SparseCore 0:
  18.3 151.8 all-reduce.2
Sparse Core Ops, SparseCore 1:
  21.9 139.3 all-gather.1
where the time goes:
time: 277 us; the launch traced here: 276 us
  waiting for transfers between devices  122 us (44%)
  local copies, waits for them, and re-layouts  69 us (25%)
  blocking collectives  40.3 us (15%)
  matrix products  18.6 us (7%)
  between operations  18 us (6%)
  other arithmetic  7.93 us (3%)
    psum x1, waiting for transfers between devices, broadcast(): return lax.psum(jnp.where(mine, x, jnp.zeros_like(x)), axis)  121 us
    all_to_all x1, blocking collectives, shards(): lax.all_to_all(outgoing.reshape(col_count, capacity, BS, BS), 'col', spli...  40.3 us
    unnamed x9, local copies, waits for them, and re-layouts  30 us
    dot_general x1, matrix products, shards(): jnp.dot(whole_rows, jnp.concatenate(panels, axis=0), preferred_element_ty...  18.6 us
    reshape x1, local copies, waits for them, and re-layouts, select_blocks(): shaped = full_tile.reshape(row_count, BS, CB_DEV, BS).transpose(0, 2, 1, 3)  12.3 us
    gather x2, local copies, waits for them, and re-layouts, select_blocks(): return jnp.take(shaped.reshape(row_count * CB_DEV, BS, BS), listed, axis=0)  9.63 us
    transpose x1, local copies, waits for them, and re-layouts, select_blocks(): shaped = full_tile.reshape(row_count, BS, CB_DEV, BS).transpose(0, 2, 1, 3)  8.91 us
  transfers between devices with their start and end apart: 2, of which 1 were waited for; matrix products, arithmetic and copies ran while one was open for 11% of the time, Pallas kernels for 0%

commit v1 on v0

v1 whole, which is shorter than its diff:
```python
import functools

import jax
import jax.numpy as jnp
from jax import lax
from jax.experimental import pallas as pl
from jax.experimental.pallas import tpu as pltpu
from jax.sharding import PartitionSpec as P

MESH = pl.DeviceIdType.MESH
BS = 128
CB = 11
RB = 16
PB = 4
DEPTH = 2048
HALF = DEPTH // 2
NCOL = 32
SHARD = 64
PARTS = 4
UNIT = SHARD // PARTS
SLOTS = 2
PANEL_CUTS = (0, 3, 6, 9, 11)
PANEL_PARTS = len(PANEL_CUTS) - 1


def kernel(
    table_ref, owners_ref, mask_ref, rows_hbm, panel_hbm, tile_hbm, out_ref,
    rows, panels, panel_in, tile, staged,
    load_sem, unit_send, unit_recv, panel_send, panel_recv, out_send, out_recv, self_sem,
):
    row = lax.axis_index("row")
    col = lax.axis_index("col")
    y, z, h = col // 8, (col // 2) % 4, col % 2
    x_lo, core = row // 2, row % 2

    def peer(dy, dz, dh):
        return ((y + dy + 4) % 4) * 8 + ((z + dz + 4) % 4) * 2 + (h + dh) % 2

    beside = (1 - x_lo) * 2 + core
    other_core = x_lo * 2 + 1 - core

    own = rows.at[col // 2, pl.ds(pl.multiple_of(h * SHARD, SHARD), SHARD)]
    loads = [
        pltpu.make_async_copy(rows_hbm, own, load_sem.at[0]),
        pltpu.make_async_copy(panel_hbm.at[0], panel_in, load_sem.at[1]),
    ]
    for c in range(CB):
        loads.append(
            pltpu.make_async_copy(
                tile_hbm.at[:, :, pl.ds(c * BS, BS)], tile.at[c], load_sem.at[2 + c]
            )
        )
    for load in loads:
        load.start()

    barrier = pltpu.get_barrier_semaphore()

    def greet(n, carry):
        pl.semaphore_signal(
            barrier, inc=1, device_id=(row, (col + n) % NCOL), device_id_type=MESH
        )
        return carry

    lax.fori_loop(1, NCOL, greet, 0)
    pl.semaphore_signal(barrier, inc=1, device_id=(beside, col), device_id_type=MESH)
    pl.semaphore_signal(barrier, inc=1, device_id=(other_core, col), device_id_type=MESH)
    pl.semaphore_wait(barrier, NCOL + 1)

    sends = []

    def unit_view(q, source, half):
        lines = pl.ds(pl.multiple_of(source % 2 * SHARD + q * UNIT, UNIT), UNIT)
        if half is None:
            return rows.at[source // 2, lines]
        return rows.at[source // 2, lines, pl.ds(half * HALF, HALF)]

    def send(q, unit, to, half=None):
        source = peer(*unit)
        view = unit_view(q, source, half)
        copy = pltpu.make_async_remote_copy(
            src_ref=view,
            dst_ref=view,
            send_sem=unit_send.at[len(sends)],
            recv_sem=unit_recv.at[q, source, half or 0],
            device_id=(row, peer(*to)),
            device_id_type=MESH,
        )
        copy.start()
        sends.append(copy)

    def arrived(q, unit, half=None):
        source = peer(*unit)
        view = unit_view(q, source, half)
        pltpu.make_async_remote_copy(
            src_ref=view,
            dst_ref=view,
            send_sem=unit_send.at[0],
            recv_sem=unit_recv.at[q, source, half or 0],
            device_id=(row, col),
            device_id_type=MESH,
        ).wait_recv()

    def along(axis, step):
        return (step, 0, 0) if axis == 0 else (0, step, 0)

    def unit_at(fast, first, second):
        return (first, second, 0) if fast == 0 else (second, first, 1)

    def both_ways(q, fast, unit, axis, half=None):
        send(q, unit, along(axis, 1), half)
        send(q, unit, along(axis, -1), half)

    def stage0(q):
        send(q, (0, 0, 0), (0, 0, 1))
        both_ways(q, 0, (0, 0, 0), 0)
        both_ways(q, 0, (0, 0, 0), 1)

    def forward(q, unit, axis, came):
        send(q, unit, along(axis, -came), 0 if came < 0 else 1)

    def stage1(q):
        arrived(q, (0, 0, 1))
        both_ways(q, 1, (0, 0, 1), 1)
        both_ways(q, 1, (0, 0, 1), 0)
        for came in (-1, 1):
            unit = unit_at(0, came, 0)
            arrived(q, unit)
            forward(q, unit, 0, came)
            both_ways(q, 0, unit, 1)

    def stage2(q):
        for came in (-1, 1):
            unit = unit_at(0, 0, came)
            arrived(q, unit)
            forward(q, unit, 1, came)
        for came in (-1, 1):
            unit = unit_at(1, came, 0)
            arrived(q, unit)
            forward(q, unit, 1, came)
            both_ways(q, 1, unit, 0)
        for came in (-1, 1):
            unit = unit_at(1, 0, came)
            arrived(q, unit)
            forward(q, unit, 0, came)

    def stage3(q):
        for fast in (0, 1):
            for half in (0, 1):
                unit = unit_at(fast, 2, 0)
                arrived(q, unit, half)
                both_ways(q, fast, unit, 1 - fast, half)
        for fast in (0, 1):
            for first in (-1, 1):
                for came in (-1, 1):
                    unit = unit_at(fast, first, came)
                    arrived(q, unit)
                    forward(q, unit, 1 - fast, came)

    def stage4(q):
        for fast in (0, 1):
            for came in (-1, 1):
                unit = unit_at(fast, 2, came)
                for half in (0, 1):
                    arrived(q, unit, half)
                forward(q, unit, 1 - fast, came)

    def stage5(q):
        for fast in (0, 1):
            for first in (0, -1, 1, 2):
                for half in (0, 1):
                    arrived(q, unit_at(fast, first, 2), half)

    panel_sends = []

    def panel_copy(part, slot, kind, to):
        first, last = PANEL_CUTS[part], PANEL_CUTS[part + 1]
        view = panels.at[slot, pl.ds(first, last - first)]
        return pltpu.make_async_remote_copy(
            src_ref=view,
            dst_ref=view,
            send_sem=panel_send.at[kind, part],
            recv_sem=panel_recv.at[kind, part],
            device_id=(to, col),
            device_id_type=MESH,
        )

    def start_panels():
        for part in range(PANEL_PARTS):
            copy = panel_copy(part, row, 0, beside)
            copy.start()
            panel_sends.append(copy)
        for part in range(PANEL_PARTS):
            copy = panel_copy(part, row, 1, other_core)
            copy.start()
            panel_sends.append(copy)

    def pass_panel(part):
        panel_copy(part, beside, 0, beside).wait_recv()
        copy = panel_copy(part, beside, 2, other_core)
        copy.start()
        panel_sends.append(copy)

    stages = [stage0, stage1, stage2, stage3, stage4, stage5]

    loads[0].wait()
    stage0(0)

    loads[1].wait()
    for p in range(PB):
        for c in range(CB):
            factor = mask_ref[0, p, c].astype(jnp.float32)
            block = panel_in[p * BS : (p + 1) * BS, c * BS : (c + 1) * BS]
            panels[row, c, p * BS : (p + 1) * BS] = (
                block.astype(jnp.float32) * factor
            ).astype(jnp.bfloat16)
    start_panels()

    for step in range(1, PARTS + len(stages) - 1):
        for q in range(PARTS):
            if 0 <= step - q < len(stages):
                stages[step - q](q)
        if step >= 4 and step - 4 < PANEL_PARTS:
            pass_panel(step - 4)
    for part in range(PANEL_PARTS):
        panel_copy(part, other_core, 1, other_core).wait_recv()
    for part in range(PANEL_PARTS):
        panel_copy(part, (1 - x_lo) * 2 + 1 - core, 2, other_core).wait_recv()
    for load in loads[2:]:
        load.wait()

    def product(slot):
        i = table_ref[0, slot]
        j = table_ref[1, slot]
        live = table_ref[2, slot].astype(jnp.float32)
        cube = jnp.zeros((BS, BS), jnp.float32)
        for k in range(4):
            cube = cube + jnp.dot(
                rows[i, :, k * PB * BS : (k + 1) * PB * BS],
                panels[owners_ref[k], j],
                preferred_element_type=jnp.float32,
            )
        square = tile[j, i].astype(jnp.float32)
        return ((3.0 * square - 2.0 * cube) * live).astype(jnp.bfloat16)

    def owner_of(n):
        return peer(n // 8, (n // 2) % 4, n % 2)

    def source_of(n):
        return peer(4 - n // 8, 4 - (n // 2) % 4, n % 2)

    def make(n):
        owner = owner_of(n)
        for s in range(SLOTS):
            staged[n, s] = product(owner * SLOTS + s)
        return owner

    def out_copy(n, owner, at):
        return pltpu.make_async_remote_copy(
            src_ref=staged.at[n],
            dst_ref=out_ref.at[pl.ds(at * SLOTS, SLOTS)],
            send_sem=out_send.at[n],
            recv_sem=out_recv.at[n],
            device_id=(row, owner),
            device_id_type=MESH,
        )

    def exchange(n, carry):
        owner = make(n)
        out_copy(n, owner, col).start()
        return carry

    lax.fori_loop(1, NCOL, exchange, 0)
    make(0)
    keep = pltpu.make_async_copy(
        staged.at[0], out_ref.at[pl.ds(col * SLOTS, SLOTS)], self_sem.at[0]
    )
    keep.start()

    for copy in sends:
        copy.wait_send()
    for copy in panel_sends:
        copy.wait_send()

    def finish(n, carry):
        out_copy(n, owner_of(n), col).wait_send()
        out_copy(n, owner_of(n), source_of(n)).wait_recv()
        return carry

    lax.fori_loop(1, NCOL, finish, 0)
    keep.wait()


def slot_table(block_ids, dest, counts):
    count = block_ids.shape[0]
    owner = dest[:, 0]
    entry = jnp.arange(count, dtype=jnp.int32)
    same = (owner[:, None] == owner[None, :]) & (entry[None, :] < entry[:, None])
    slot = owner * SLOTS + jnp.sum(same.astype(jnp.int32), axis=1)
    live = (entry < counts[0]).astype(jnp.int32)
    block_row = block_ids // CB
    values = jnp.stack([block_row, block_ids - block_row * CB, live])
    at = slot[None, :] == jnp.arange(NCOL * SLOTS, dtype=jnp.int32)[:, None]
    return jnp.sum(jnp.where(at[None], values[:, None, :], 0), axis=2)


def shards(x2_rows, x_panels, panel_mask, owners, x2_tile, block_ids, dest, counts):
    sem = pltpu.SemaphoreType.DMA
    return pl.pallas_call(
        kernel,
        out_shape=jax.ShapeDtypeStruct((NCOL * SLOTS, BS, BS), jnp.bfloat16),
        in_specs=[pl.BlockSpec(memory_space=pltpu.SMEM)] * 3
        + [pl.BlockSpec(memory_space=pl.ANY)] * 3,
        out_specs=pl.BlockSpec(memory_space=pl.ANY),
        scratch_shapes=[
            pltpu.VMEM((RB, BS, DEPTH), jnp.bfloat16),
            pltpu.VMEM((4, CB, PB * BS, BS), jnp.bfloat16),
            pltpu.VMEM((PB * BS, CB * BS), jnp.bfloat16),
            pltpu.VMEM((CB, RB, BS, BS), jnp.bfloat16),
            pltpu.VMEM((NCOL, SLOTS, BS, BS), jnp.bfloat16),
            sem((2 + CB,)),
            sem((PARTS * 56,)),
            sem((PARTS, NCOL, 2)),
            sem((3, PANEL_PARTS)),
            sem((3, PANEL_PARTS)),
            sem((NCOL,)),
            sem((NCOL,)),
            sem((1,)),
        ],
        compiler_params=pltpu.CompilerParams(
            collective_id=0, has_side_effects=True, vmem_limit_bytes=48 * 2**20
        ),
        cost_estimate=pl.CostEstimate(
            flops=4_300_000_000, bytes_accessed=12_000_000, transcendentals=0
        ),
    )(
        slot_table(block_ids, dest, counts),
        owners,
        panel_mask,
        x2_rows,
        x_panels,
        x2_tile.reshape(RB, BS, CB * BS),
    )


def solution(mesh):
    return jax.shard_map(
        shards,
        mesh=mesh,
        in_specs=(
            P(("row", "col"), None),
            P("row", None, "col"),
            P("row", None, "col"),
            P(),
            P("row", "col"),
            P(("row", "col")),
            P(("row", "col"), None),
            P(("row", "col")),
        ),
        out_specs=P(("row", "col"), None, None),
        check_vma=False,
    )
```

time: 277 us -> 130 us (0.47)
  waiting for transfers between devices: 122 us -> 0 us
  Pallas kernels: 0 us -> 121 us
  local copies, waits for them, and re-layouts: 69 us -> 4.97 us
  blocking collectives: 40.3 us -> 0 us
  matrix products: 18.6 us -> 0 us
  between operations: 18 us -> 0.69 us
  other arithmetic: 7.93 us -> 2.44 us
    pallas_call x0 -> x1, Pallas kernels: none -> 121 us  [shards(): pl.pallas_call(kernel, out_shape=jax.ShapeDtypeStruct((NCOL * SLOTS, BS,...]
    psum x1 -> x0, waiting for transfers between devices: 121 us -> none  [broadcast(): return lax.psum(jnp.where(mine, x, jnp.zeros_like(x)), axis)]
    all_to_all x1 -> x0, blocking collectives: 40.3 us -> none  [shards(): lax.all_to_all(outgoing.reshape(col_count, capacity, BS, BS), 'col', spli...]
    unnamed x9, local copies, waits for them, and re-layouts: 30 us -> 4.97 us
    dot_general x1 -> x0, matrix products: 18.6 us -> none  [shards(): jnp.dot(whole_rows, jnp.concatenate(panels, axis=0), preferred_element_ty...]
    reshape x1 -> x0, local copies, waits for them, and re-layouts: 12.3 us -> none  [select_blocks(): shaped = full_tile.reshape(row_count, BS, CB_DEV, BS).transpose(0, 2, 1, 3)]
    gather x2 -> x0, local copies, waits for them, and re-layouts: 9.63 us -> none  [select_blocks(): return jnp.take(shaped.reshape(row_count * CB_DEV, BS, BS), listed, axis=0)]
    transpose x1 -> x0, local copies, waits for them, and re-layouts: 8.91 us -> none  [select_blocks(): shaped = full_tile.reshape(row_count, BS, CB_DEV, BS).transpose(0, 2, 1, 3)]
  transfers between devices with their start and end apart: 2 -> 0, of which waited for: 1 -> 0; matrix products, arithmetic and copies ran while one was open for 11% -> 0% of each run, Pallas kernels for 0% -> 0%
where the time goes in v1:
time: 130 us; the launch traced here: 129 us
  Pallas kernels  121 us (93%)
  local copies, waits for them, and re-layouts  4.97 us (4%)
  other arithmetic  2.44 us (2%)
    pallas_call x1, Pallas kernels, shards(): pl.pallas_call(kernel, out_shape=jax.ShapeDtypeStruct((NCOL * SLOTS, BS,...  121 us
    unnamed x9, local copies, waits for them, and re-layouts  4.97 us

profile of v1, /device:TPU:0, one launch (start us, length us, event | category | flops | bytes accessed | tf_op | source)
XLA Modules:
  0.0 129.3 jit_solution(7341585995694867671)
XLA Ops:
  0.7 0.9 convert_reduce_fusion
  1.6 0.7 multiply_add_fusion
  2.2 0.7 subtract_bitcast_fusion
  2.9 0.1 iota_compare_fusion
  3.0 0.1 select_reduce_fusion.table_ref
  3.1 0.0 copy-start
  3.1 1.4 %copy-done = bf16[1,512,1408]{2,1,0:T(8,128)(2,1)S(1)} copy-done((bf16[1,512,1408]{2,1,0:T(8,128)(2,1)S(1)}, bf16[1,512,1408]{2,1,0:T(8,128)(2,1)}, u32[]{:S(2)}) %copy-start) | copy-done | bytes 1441816
  4.5 0.0 copy-start.1
  4.5 0.9 copy-done.1
  5.4 0.0 copy-start.2
  5.4 0.7 copy-done.2
  6.1 0.0 copy-start.3
  6.1 0.7 copy-done.3
  6.8 121.3 %shard_map.82 = bf16[64,128,128]{2,1,0:T(8,128)(2,1)S(1)} custom-call(s32[3,64]{1,0:T(4,128)S(1)} %select_reduce_fusion.table_ref, s32[4]{0:T(128)S(1)} %copy-done.3, s32[1,4,11]{2,1,0:T(4,128)S(1)} %copy-done.2, bf16[64,2048]{1,0:T(8,128)(2,1)S(1)} %copy-done.1, bf16[1,512,1408]{2,1,0:T(8,128)(2,1)S(1)} %copy-done, bf16[16,128,1408]{2,1,0:T(8,128)(2,1)} %bitcast.9), custom_call_target="tpu_custom_call" | custom-call | flops 4300000256 | bytes 12000000 | tf_op jit(solution)/shard_map/pallas_call | solution.py:308
  128.0 1.3 %copy.11 = bf16[64,128,128]{2,1,0:T(8,128)(2,1)} copy(bf16[64,128,128]{2,1,0:T(8,128)(2,1)S(1)} %shard_map.82) | data formatting | bytes 4194304
  (2 shorter events, 0.0 us)
Async XLA Ops:
  3.1 1.4 %copy-start = (bf16[1,512,1408]{2,1,0:T(8,128)(2,1)S(1)}, bf16[1,512,1408]{2,1,0:T(8,128)(2,1)}, u32[]{:S(2)}) copy-start(bf16[1,512,1408]{2,1,0:T(8,128)(2,1)} %panel_hbm.1) | copy-start | bytes 4325380
  4.5 0.9 copy-start.1
  5.4 0.7 copy-start.2
  6.1 0.7 copy-start.3

commit v2 on v1

v2 whole, which is shorter than its diff:
```python
import functools

import jax
import jax.numpy as jnp
from jax import lax
from jax.experimental import pallas as pl
from jax.experimental.pallas import tpu as pltpu
from jax.sharding import PartitionSpec as P

MESH = pl.DeviceIdType.MESH
BS = 128
CB = 11
RB = 16
PB = 4
DEPTH = 2048
HALF = DEPTH // 2
NCOL = 32
SHARD = 64
PARTS = 1
UNIT = SHARD // PARTS
SLOTS = 2
PANEL_CUTS = (0, 3, 6, 9, 11)
PANEL_PARTS = len(PANEL_CUTS) - 1


def kernel(
    ids_hbm, dest_hbm, counts_hbm, owners_hbm, mask_hbm, rows_hbm, panel_hbm, tile_hbm, out_ref,
    rows, panels, panel_in, tile, staged, ids, dest, table,
    counts_ref, owners_ref, mask_ref, table_ref,
    load_sem, ring_send, pair_send, pair_recv, unit_recv, panel_send, panel_recv, out_send, out_recv,
):
    row = lax.axis_index("row")
    col = lax.axis_index("col")
    y, z, h = col // 8, (col // 2) % 4, col % 2
    x_lo, core = row // 2, row % 2

    def peer(dy, dz, dh):
        return ((y + dy + 4) % 4) * 8 + ((z + dz + 4) % 4) * 2 + (h + dh) % 2

    beside = (1 - x_lo) * 2 + core
    other_core = x_lo * 2 + 1 - core

    own = rows.at[col // 2, pl.ds(pl.multiple_of(h * SHARD, SHARD), SHARD)]
    loads = [
        pltpu.make_async_copy(rows_hbm, own, load_sem.at[0]),
        pltpu.make_async_copy(panel_hbm.at[0], panel_in, load_sem.at[1]),
        pltpu.make_async_copy(mask_hbm, mask_ref, load_sem.at[2]),
        pltpu.make_async_copy(owners_hbm, owners_ref, load_sem.at[3]),
        pltpu.make_async_copy(counts_hbm, counts_ref, load_sem.at[4]),
        pltpu.make_async_copy(ids_hbm, ids, load_sem.at[5]),
        pltpu.make_async_copy(dest_hbm, dest, load_sem.at[6]),
    ]
    for c in range(CB):
        loads.append(
            pltpu.make_async_copy(
                tile_hbm.at[:, :, pl.ds(c * BS, BS)], tile.at[c], load_sem.at[7 + c]
            )
        )
    for load in loads:
        load.start()

    barrier = pltpu.get_barrier_semaphore()

    def greet(n, carry):
        pl.semaphore_signal(
            barrier, inc=1, device_id=(row, (col + n) % NCOL), device_id_type=MESH
        )
        return carry

    lax.fori_loop(1, NCOL, greet, 0)
    pl.semaphore_signal(barrier, inc=1, device_id=(beside, col), device_id_type=MESH)
    pl.semaphore_signal(barrier, inc=1, device_id=(other_core, col), device_id_type=MESH)
    pl.semaphore_wait(barrier, NCOL + 1)

    def fill_table():
        count = ids.shape[1]
        first = lax.broadcasted_iota(jnp.int32, (count, count), 0)
        second = lax.broadcasted_iota(jnp.int32, (count, count), 1)

        def upright(line):
            return jnp.sum(jnp.where(first == second, line, 0), axis=1, keepdims=True)

        owner, listed = upright(dest[...]), upright(ids[...])
        before = (owner == dest[...]) & (second < first)
        slot = owner * SLOTS + jnp.sum(before.astype(jnp.int32), axis=1, keepdims=True)
        hit = slot == lax.broadcasted_iota(jnp.int32, (count, table.shape[1]), 1)
        block_row = (listed * 745) >> 13
        entry = lax.broadcasted_iota(jnp.int32, (count, 1), 0)
        live = (entry < counts_ref[0]).astype(jnp.int32)
        table[...] = jnp.zeros_like(table)
        for n, column in enumerate((block_row, listed - block_row * CB, live)):
            table[n : n + 1] = jnp.sum(jnp.where(hit, column, 0), axis=0, keepdims=True)
        copy = pltpu.make_async_copy(table, table_ref, load_sem.at[0])
        copy.start()
        copy.wait()

    def place(unit):
        q, fast, first, second, dh = unit
        return peer(first, second, dh) if fast == 0 else peer(second, first, dh)

    def unit_view(unit, half):
        source = place(unit)
        width = HALF if half is None else HALF // 2
        start = unit[1] * HALF + (half or 0) * width
        lines = pl.ds(pl.multiple_of(source % 2 * SHARD + unit[0] * UNIT, UNIT), UNIT)
        return rows.at[source // 2, lines, pl.ds(start, width)]

    def unit_copy(unit, half, to):
        view = unit_view(unit, half)
        return pltpu.make_async_remote_copy(
            src_ref=view,
            dst_ref=view,
            send_sem=ring_send.at[0],
            recv_sem=unit_recv.at[unit[0], unit[1], place(unit), half or 0],
            device_id=(row, to),
            device_id_type=MESH,
        )

    def arrived(unit, half=None):
        unit_copy(unit, half, col).wait_recv()

    def along(axis, step):
        return peer(step, 0, 0) if axis == 0 else peer(0, step, 0)

    def both_ways(unit, axis, half=None):
        unit_copy(unit, half, along(axis, 1)).start()
        unit_copy(unit, half, along(axis, -1)).start()

    def forward(unit, axis, came):
        unit_copy(unit, 0 if came < 0 else 1, along(axis, -came)).start()

    def pair_copy(q, source):
        lines = pl.ds(pl.multiple_of(source % 2 * SHARD + q * UNIT, UNIT), UNIT)
        view = rows.at[source // 2, lines]
        return pltpu.make_async_remote_copy(
            src_ref=view,
            dst_ref=view,
            send_sem=pair_send.at[0],
            recv_sem=pair_recv.at[q],
            device_id=(row, peer(0, 0, 1)),
            device_id_type=MESH,
        )

    def stage0(q, dh):
        if dh:
            pair_copy(q, peer(0, 0, 1)).wait_recv()
        for fast in (0, 1):
            both_ways((q, fast, 0, 0, dh), fast)
        for fast in (0, 1):
            both_ways((q, fast, 0, 0, dh), 1 - fast)

    def stage1(q, dh):
        for came in (-1, 1):
            for fast in (0, 1):
                unit = (q, fast, came, 0, dh)
                arrived(unit)
                forward(unit, fast, came)
                both_ways(unit, 1 - fast)

    def stage2(q, dh):
        for came in (-1, 1):
            for fast in (0, 1):
                unit = (q, fast, 0, came, dh)
                arrived(unit)
                forward(unit, 1 - fast, came)
        for half in (0, 1):
            for fast in (0, 1):
                unit = (q, fast, 2, 0, dh)
                arrived(unit, half)
                both_ways(unit, 1 - fast, half)

    def stage3(q, dh):
        for first in (-1, 1):
            for came in (-1, 1):
                for fast in (0, 1):
                    unit = (q, fast, first, came, dh)
                    arrived(unit)
                    forward(unit, 1 - fast, came)

    def stage4(q, dh):
        for came in (-1, 1):
            for fast in (0, 1):
                unit = (q, fast, 2, came, dh)
                arrived(unit, 0)
                arrived(unit, 1)
                forward(unit, 1 - fast, came)

    def stage5(q, dh):
        for first in (0, -1, 1, 2):
            for fast in (0, 1):
                arrived((q, fast, first, 2, dh), 0)
                arrived((q, fast, first, 2, dh), 1)

    def panel_copy(part, slot, kind, to):
        first, last = PANEL_CUTS[part], PANEL_CUTS[part + 1]
        view = panels.at[slot, pl.ds(first, last - first)]
        return pltpu.make_async_remote_copy(
            src_ref=view,
            dst_ref=view,
            send_sem=panel_send.at[kind],
            recv_sem=panel_recv.at[kind, part],
            device_id=(to, col),
            device_id_type=MESH,
        )

    def start_panels():
        for part in range(PANEL_PARTS):
            panel_copy(part, row, 0, beside).start()

    def pass_panel(part):
        panel_copy(part, beside, 0, beside).wait_recv()
        panel_copy(part, beside, 2, other_core).start()

    loads[0].wait()
    for q in range(PARTS):
        pair_copy(q, col).start()
    for q in range(PARTS):
        stage0(q, 0)

    for load in loads[1:7]:
        load.wait()
    fill_table()
    for p in range(PB):
        for c in range(CB):
            factor = mask_ref[0, p, c].astype(jnp.float32)
            block = panel_in[p * BS : (p + 1) * BS, c * BS : (c + 1) * BS]
            panels[row, c, p * BS : (p + 1) * BS] = (
                block.astype(jnp.float32) * factor
            ).astype(jnp.bfloat16)
    for part in range(PANEL_PARTS):
        panel_copy(part, row, 1, other_core).start()
    for q in range(PARTS):
        stage0(q, 1)
    start_panels()
    for stage in (stage1, stage2, stage3, stage4):
        for dh in (0, 1):
            for q in range(PARTS):
                stage(q, dh)
    for part in range(PANEL_PARTS):
        pass_panel(part)
    for dh in (0, 1):
        for q in range(PARTS):
            stage5(q, dh)
    for part in range(PANEL_PARTS):
        panel_copy(part, other_core, 1, other_core).wait_recv()
    for part in range(PANEL_PARTS):
        panel_copy(part, (1 - x_lo) * 2 + 1 - core, 2, other_core).wait_recv()
    for load in loads[7:]:
        load.wait()

    def product(slot):
        i = table_ref[0, slot]
        j = table_ref[1, slot]
        live = table_ref[2, slot].astype(jnp.float32)
        cube = jnp.zeros((BS, BS), jnp.float32)
        for k in range(4):
            cube = cube + jnp.dot(
                rows[i, :, k * PB * BS : (k + 1) * PB * BS],
                panels[owners_ref[k], j],
                preferred_element_type=jnp.float32,
            )
        square = tile[j, i].astype(jnp.float32)
        return ((3.0 * square - 2.0 * cube) * live).astype(jnp.bfloat16)

    def owner_of(n):
        mixed = n * 11 % NCOL
        return peer(mixed // 8, mixed // 2 % 4, mixed % 2)

    def make(n):
        owner = owner_of(n)
        for s in range(SLOTS):
            staged[n, s] = product(owner * SLOTS + s)
        return owner

    mine = out_ref.at[pl.ds(col * SLOTS, SLOTS)]

    def give(n, owner):
        pltpu.make_async_remote_copy(
            src_ref=staged.at[n],
            dst_ref=mine,
            send_sem=out_send.at[0],
            recv_sem=out_recv.at[0],
            device_id=(row, owner),
            device_id_type=MESH,
        ).start()

    def exchange(pair, carry):
        n = 2 * pair + 1
        first, second = make(n), make(n + 1)
        give(n, first)
        give(n + 1, second)
        return carry

    lax.fori_loop(0, NCOL // 2 - 1, exchange, 0)
    last = make(NCOL - 1)
    make(0)
    give(NCOL - 1, last)
    keep = pltpu.make_async_copy(staged.at[0], mine, load_sem.at[1])
    keep.start()

    def await_bytes(ref, sem):
        pltpu.make_async_copy(ref, ref, sem).wait()

    await_bytes(rows.at[pl.ds(0, RB - 1)], ring_send.at[0])
    await_bytes(own, pair_send.at[0])
    for kind in range(3):
        await_bytes(panels.at[0], panel_send.at[kind])
    keep.wait()
    await_bytes(staged.at[pl.ds(1, NCOL - 1)], out_send.at[0])
    await_bytes(staged.at[pl.ds(1, NCOL - 1)], out_recv.at[0])


def shards(x2_rows, x_panels, panel_mask, owners, x2_tile, block_ids, dest, counts):
    sem = pltpu.SemaphoreType.DMA
    count = block_ids.shape[0]
    return pl.pallas_call(
        kernel,
        out_shape=jax.ShapeDtypeStruct((NCOL * SLOTS, BS, BS), jnp.bfloat16),
        in_specs=[pl.BlockSpec(memory_space=pltpu.HBM)] * 8,
        out_specs=pl.BlockSpec(memory_space=pl.ANY),
        scratch_shapes=[
            pltpu.VMEM((RB, BS, DEPTH), jnp.bfloat16),
            pltpu.VMEM((4, CB, PB * BS, BS), jnp.bfloat16),
            pltpu.VMEM((PB * BS, CB * BS), jnp.bfloat16),
            pltpu.VMEM((CB, RB, BS, BS), jnp.bfloat16),
            pltpu.VMEM((NCOL, SLOTS, BS, BS), jnp.bfloat16),
            pltpu.VMEM((1, count), jnp.int32),
            pltpu.VMEM((1, count), jnp.int32),
            pltpu.VMEM((8, BS), jnp.int32),
            pltpu.SMEM(counts.shape, jnp.int32),
            pltpu.SMEM(owners.shape, jnp.int32),
            pltpu.SMEM(panel_mask.shape, jnp.int32),
            pltpu.SMEM((8, BS), jnp.int32),
            sem((7 + CB,)),
            sem((1,)),
            sem((1,)),
            sem((PARTS,)),
            sem((PARTS, 2, NCOL, 2)),
            sem((3,)),
            sem((3, PANEL_PARTS)),
            sem((1,)),
            sem((1,)),
        ],
        compiler_params=pltpu.CompilerParams(
            collective_id=0, has_side_effects=True, vmem_limit_bytes=60 * 2**20
        ),
        cost_estimate=pl.CostEstimate(
            flops=4_300_000_000, bytes_accessed=12_000_000, transcendentals=0
        ),
    )(
        block_ids.reshape(1, count),
        dest.reshape(1, count),
        counts,
        owners,
        panel_mask,
        x2_rows,
        x_panels,
        x2_tile.reshape(RB, BS, CB * BS),
    )


def solution(mesh):
    return jax.shard_map(
        shards,
        mesh=mesh,
        in_specs=(
            P(("row", "col"), None),
            P("row", None, "col"),
            P("row", None, "col"),
            P(),
            P("row", "col"),
            P(("row", "col")),
            P(("row", "col"), None),
            P(("row", "col")),
        ),
        out_specs=P(("row", "col"), None, None),
        check_vma=False,
    )
```

time: 130 us -> 86.7 us (0.67)
  Pallas kernels: 121 us -> 82.7 us
  other arithmetic: 2.44 us -> 0 us
  local copies, waits for them, and re-layouts: 4.97 us -> 3.16 us
    pallas_call x1, Pallas kernels: 121 us -> 82.7 us  [shards(): pl.pallas_call(kernel, out_shape=jax.ShapeDtypeStruct((NCOL * SLOTS, BS,...]
    unnamed x9 -> x1, local copies, waits for them, and re-layouts: 4.97 us -> 3.16 us
where the time goes in v2:
time: 86.7 us; the launch traced here: 86.5 us
  Pallas kernels  82.7 us (95%)
  local copies, waits for them, and re-layouts  3.16 us (4%)
    pallas_call x1, Pallas kernels, shards(): pl.pallas_call(kernel, out_shape=jax.ShapeDtypeStruct((NCOL * SLOTS, BS,...  82.7 us
    unnamed x1, local copies, waits for them, and re-layouts  3.16 us

profile of v2, /device:TPU:0, one launch (start us, length us, event | category | flops | bytes accessed | tf_op | source)
XLA Modules:
  0.0 86.5 jit_solution(10717894385518709670)
XLA Ops:
  0.7 82.7 %shard_map.82 = bf16[64,128,128]{2,1,0:T(8,128)(2,1)} custom-call(s32[1,48]{1,0:T(1,128)} %bitcast.4, s32[1,48]{1,0:T(1,128)} %bitcast.5, s32[1]{0:T(128)S(6)} %copy.10.counts_hbm, s32[4]{0:T(128)} %owners_hbm.1, s32[1,4,11]{2,1,0:T(4,128)} %mask_hbm.1, bf16[64,2048]{1,0:T(8,128)(2,1)} %rows_hbm.1, bf16[1,512,1408]{2,1,0:T(8,128)(2,1)} %panel_hbm.1, ...), custom_call_target="tpu_custom_call" | custom-call | flops 4300000256 | bytes 12000000 | tf_op jit(solution)/shard_map/pallas_call | solution.py:316
  83.4 3.2 %copy.11 = bf16[64,128,128]{2,1,0:T(8,128)(2,1)} copy(bf16[64,128,128]{2,1,0:T(8,128)(2,1)} %shard_map.82) | data formatting | bytes 4194304

commit v3 on v2

--- a/solution.py
+++ b/solution.py
@@ -27,7 +27,7 @@
     ids_hbm, dest_hbm, counts_hbm, owners_hbm, mask_hbm, rows_hbm, panel_hbm, tile_hbm, out_ref,
     rows, panels, panel_in, tile, staged, ids, dest, table,
     counts_ref, owners_ref, mask_ref, table_ref,
-    load_sem, ring_send, pair_send, pair_recv, unit_recv, panel_send, panel_recv, out_send, out_recv,
+    load_sem, tile_sem, ring_send, pair_send, pair_recv, unit_recv, stay_recv, panel_send, panel_recv, out_send, out_recv,
 ):
     row = lax.axis_index("row")
     col = lax.axis_index("col")
@@ -41,23 +41,8 @@
     other_core = x_lo * 2 + 1 - core
 
     own = rows.at[col // 2, pl.ds(pl.multiple_of(h * SHARD, SHARD), SHARD)]
-    loads = [
-        pltpu.make_async_copy(rows_hbm, own, load_sem.at[0]),
-        pltpu.make_async_copy(panel_hbm.at[0], panel_in, load_sem.at[1]),
-        pltpu.make_async_copy(mask_hbm, mask_ref, load_sem.at[2]),
-        pltpu.make_async_copy(owners_hbm, owners_ref, load_sem.at[3]),
-        pltpu.make_async_copy(counts_hbm, counts_ref, load_sem.at[4]),
-        pltpu.make_async_copy(ids_hbm, ids, load_sem.at[5]),
-        pltpu.make_async_copy(dest_hbm, dest, load_sem.at[6]),
-    ]
-    for c in range(CB):
-        loads.append(
-            pltpu.make_async_copy(
-                tile_hbm.at[:, :, pl.ds(c * BS, BS)], tile.at[c], load_sem.at[7 + c]
-            )
-        )
-    for load in loads:
-        load.start()
+    load_rows = pltpu.make_async_copy(rows_hbm, own, load_sem.at[0])
+    load_rows.start()
 
     barrier = pltpu.get_barrier_semaphore()
 
@@ -70,7 +55,30 @@
     lax.fori_loop(1, NCOL, greet, 0)
     pl.semaphore_signal(barrier, inc=1, device_id=(beside, col), device_id_type=MESH)
     pl.semaphore_signal(barrier, inc=1, device_id=(other_core, col), device_id_type=MESH)
+
+    loads = [
+        pltpu.make_async_copy(source, target, load_sem.at[n + 1])
+        for n, (source, target) in enumerate(
+            (
+                (dest_hbm, dest),
+                (ids_hbm, ids),
+                (counts_hbm, counts_ref),
+                (mask_hbm, mask_ref),
+                (owners_hbm, owners_ref),
+                (panel_hbm.at[0], panel_in),
+            )
+        )
+    ]
+    for load in loads:
+        load.start()
+    for c in range(CB):
+        pltpu.make_async_copy(
+            tile_hbm.at[:, :, pl.ds(c * BS, BS)], tile.at[c], tile_sem.at[0]
+        ).start()
     pl.semaphore_wait(barrier, NCOL + 1)
+
+    def await_bytes(ref, sem):
+        pltpu.make_async_copy(ref, ref, sem).wait()
 
     def fill_table():
         count = ids.shape[1]
@@ -105,29 +113,46 @@
         lines = pl.ds(pl.multiple_of(source % 2 * SHARD + unit[0] * UNIT, UNIT), UNIT)
         return rows.at[source // 2, lines, pl.ds(start, width)]
 
-    def unit_copy(unit, half, to):
+    def unit_sem(unit, half):
+        q, fast, first, second, dh = unit
+        if second == 2 or (first == 2 and second and half != (0 if second < 0 else 1)):
+            return stay_recv.at[0]
+        kind = [
+            (-1, 0, None), (1, 0, None), (0, -1, None), (0, 1, None),
+            (2, 0, 0), (2, 0, 1), (2, -1, 0), (2, 1, 1),
+            (-1, -1, None), (-1, 1, None), (1, -1, None), (1, 1, None),
+        ].index((first, second, half))
+        return unit_recv.at[((q * 2 + dh) * 2 + fast) * 12 + kind]
+
+    def unit_copy(unit, half, arrives, to):
         view = unit_view(unit, half)
         return pltpu.make_async_remote_copy(
             src_ref=view,
             dst_ref=view,
             send_sem=ring_send.at[0],
-            recv_sem=unit_recv.at[unit[0], unit[1], place(unit), half or 0],
+            recv_sem=unit_sem(arrives, half),
             device_id=(row, to),
             device_id_type=MESH,
         )
 
     def arrived(unit, half=None):
-        unit_copy(unit, half, col).wait_recv()
-
-    def along(axis, step):
-        return peer(step, 0, 0) if axis == 0 else peer(0, step, 0)
+        unit_copy(unit, half, unit, col).wait_recv()
+
+    def send(unit, axis, step, half=None):
+        q, fast, first, second, dh = unit
+        if axis == fast:
+            first = (first - step + 1) % 4 - 1
+        else:
+            second = (second - step + 1) % 4 - 1
+        to = peer(step, 0, 0) if axis == 0 else peer(0, step, 0)
+        unit_copy(unit, half, (q, fast, first, second, dh), to).start()
 
     def both_ways(unit, axis, half=None):
-        unit_copy(unit, half, along(axis, 1)).start()
-        unit_copy(unit, half, along(axis, -1)).start()
+        send(unit, axis, 1, half)
+        send(unit, axis, -1, half)
 
     def forward(unit, axis, came):
-        unit_copy(unit, 0 if came < 0 else 1, along(axis, -came)).start()
+        send(unit, axis, -came, 0 if came < 0 else 1)
 
     def pair_copy(q, source):
         lines = pl.ds(pl.multiple_of(source % 2 * SHARD + q * UNIT, UNIT), UNIT)
@@ -181,15 +206,8 @@
         for came in (-1, 1):
             for fast in (0, 1):
                 unit = (q, fast, 2, came, dh)
-                arrived(unit, 0)
-                arrived(unit, 1)
+                arrived(unit, 0 if came < 0 else 1)
                 forward(unit, 1 - fast, came)
-
-    def stage5(q, dh):
-        for first in (0, -1, 1, 2):
-            for fast in (0, 1):
-                arrived((q, fast, first, 2, dh), 0)
-                arrived((q, fast, first, 2, dh), 1)
 
     def panel_copy(part, slot, kind, to):
         first, last = PANEL_CUTS[part], PANEL_CUTS[part + 1]
@@ -198,7 +216,7 @@
             src_ref=view,
             dst_ref=view,
             send_sem=panel_send.at[kind],
-            recv_sem=panel_recv.at[kind, part],
+            recv_sem=panel_recv.at[part if kind == 0 else PANEL_PARTS + kind - 1],
             device_id=(to, col),
             device_id_type=MESH,
         )
@@ -211,42 +229,46 @@
         panel_copy(part, beside, 0, beside).wait_recv()
         panel_copy(part, beside, 2, other_core).start()
 
-    loads[0].wait()
+    load_rows.wait()
     for q in range(PARTS):
         pair_copy(q, col).start()
     for q in range(PARTS):
         stage0(q, 0)
 
-    for load in loads[1:7]:
+    for load in loads:
         load.wait()
     fill_table()
-    for p in range(PB):
-        for c in range(CB):
+
+    def masked(c, carry):
+        column = pl.ds(pl.multiple_of(c * BS, BS), BS)
+        for p in range(PB):
             factor = mask_ref[0, p, c].astype(jnp.float32)
-            block = panel_in[p * BS : (p + 1) * BS, c * BS : (c + 1) * BS]
+            block = panel_in[p * BS : (p + 1) * BS, column]
             panels[row, c, p * BS : (p + 1) * BS] = (
                 block.astype(jnp.float32) * factor
             ).astype(jnp.bfloat16)
+        return carry
+
+    lax.fori_loop(0, CB, masked, 0)
     for part in range(PANEL_PARTS):
         panel_copy(part, row, 1, other_core).start()
-    for q in range(PARTS):
-        stage0(q, 1)
+    stage1(0, 0)
+    stage0(0, 1)
     start_panels()
-    for stage in (stage1, stage2, stage3, stage4):
-        for dh in (0, 1):
-            for q in range(PARTS):
-                stage(q, dh)
-    for part in range(PANEL_PARTS):
+    stage1(0, 1)
+    stage2(0, 0)
+    stage2(0, 1)
+    stage3(0, 0)
+    stage4(0, 0)
+    stage3(0, 1)
+    for part in range(PANEL_PARTS - 1):
         pass_panel(part)
-    for dh in (0, 1):
-        for q in range(PARTS):
-            stage5(q, dh)
-    for part in range(PANEL_PARTS):
-        panel_copy(part, other_core, 1, other_core).wait_recv()
-    for part in range(PANEL_PARTS):
-        panel_copy(part, (1 - x_lo) * 2 + 1 - core, 2, other_core).wait_recv()
-    for load in loads[7:]:
-        load.wait()
+    stage4(0, 1)
+    pass_panel(PANEL_PARTS - 1)
+    await_bytes(rows.at[pl.ds(0, 5)], stay_recv.at[0])
+    await_bytes(panels.at[0], panel_recv.at[PANEL_PARTS])
+    await_bytes(panels.at[0], panel_recv.at[PANEL_PARTS + 1])
+    await_bytes(tile, tile_sem.at[0])
 
     def product(slot):
         i = table_ref[0, slot]
@@ -263,7 +285,7 @@
         return ((3.0 * square - 2.0 * cube) * live).astype(jnp.bfloat16)
 
     def owner_of(n):
-        mixed = n * 11 % NCOL
+        mixed = n * 5 % NCOL
         return peer(mixed // 8, mixed // 2 % 4, mixed % 2)
 
     def make(n):
@@ -285,21 +307,17 @@
         ).start()
 
     def exchange(pair, carry):
-        n = 2 * pair + 1
+        n = 2 * pair + 2
         first, second = make(n), make(n + 1)
         give(n, first)
         give(n + 1, second)
         return carry
 
+    give(1, make(1))
     lax.fori_loop(0, NCOL // 2 - 1, exchange, 0)
-    last = make(NCOL - 1)
     make(0)
-    give(NCOL - 1, last)
-    keep = pltpu.make_async_copy(staged.at[0], mine, load_sem.at[1])
+    keep = pltpu.make_async_copy(staged.at[0], mine, tile_sem.at[0])
     keep.start()
-
-    def await_bytes(ref, sem):
-        pltpu.make_async_copy(ref, ref, sem).wait()
 
     await_bytes(rows.at[pl.ds(0, RB - 1)], ring_send.at[0])
     await_bytes(own, pair_send.at[0])
@@ -331,13 +349,15 @@
             pltpu.SMEM(owners.shape, jnp.int32),
             pltpu.SMEM(panel_mask.shape, jnp.int32),
             pltpu.SMEM((8, BS), jnp.int32),
-            sem((7 + CB,)),
+            sem((7,)),
+            sem((1,)),
             sem((1,)),
             sem((1,)),
             sem((PARTS,)),
-            sem((PARTS, 2, NCOL, 2)),
+            sem((PARTS * 48,)),
+            sem((1,)),
             sem((3,)),
-            sem((3, PANEL_PARTS)),
+            sem((PANEL_PARTS + 2,)),
             sem((1,)),
             sem((1,)),
         ],

time: 86.7 us -> 84.6 us (0.976)
  Pallas kernels: 82.7 us -> 80.2 us
    pallas_call x1, Pallas kernels: 82.7 us -> 80.2 us  [shards(): pl.pallas_call(kernel, out_shape=jax.ShapeDtypeStruct((NCOL * SLOTS, BS,...]
where the time goes in v3:
time: 84.6 us; the launch traced here: 84 us
  Pallas kernels  80.2 us (95%)
  local copies, waits for them, and re-layouts  3.16 us (4%)
    pallas_call x1, Pallas kernels, shards(): pl.pallas_call(kernel, out_shape=jax.ShapeDtypeStruct((NCOL * SLOTS, BS,...  80.2 us
    unnamed x1, local copies, waits for them, and re-layouts  3.16 us

profile of v3, /device:TPU:0, one launch (start us, length us, event | category | flops | bytes accessed | tf_op | source)
XLA Modules:
  0.0 84.0 jit_solution(11343560835277234047)
XLA Ops:
  0.7 80.2 %shard_map.82 = bf16[64,128,128]{2,1,0:T(8,128)(2,1)} custom-call(s32[1,48]{1,0:T(1,128)} %bitcast.4, s32[1,48]{1,0:T(1,128)} %bitcast.5, s32[1]{0:T(128)S(6)} %copy.10.counts_hbm, s32[4]{0:T(128)} %owners_hbm.1, s32[1,4,11]{2,1,0:T(4,128)} %mask_hbm.1, bf16[64,2048]{1,0:T(8,128)(2,1)} %rows_hbm.1, bf16[1,512,1408]{2,1,0:T(8,128)(2,1)} %panel_hbm.1, ...), custom_call_target="tpu_custom_call" | custom-call | flops 4300000256 | bytes 12000000 | tf_op jit(solution)/shard_map/pallas_call | solution.py:334
  80.8 3.2 %copy.11 = bf16[64,128,128]{2,1,0:T(8,128)(2,1)} copy(bf16[64,128,128]{2,1,0:T(8,128)(2,1)} %shard_map.82) | data formatting | bytes 4194304

commit v4 on v3

--- a/solution.py
+++ b/solution.py
@@ -16,8 +16,6 @@
 HALF = DEPTH // 2
 NCOL = 32
 SHARD = 64
-PARTS = 1
-UNIT = SHARD // PARTS
 SLOTS = 2
 PANEL_CUTS = (0, 3, 6, 9, 11)
 PANEL_PARTS = len(PANEL_CUTS) - 1
@@ -40,9 +38,18 @@
     beside = (1 - x_lo) * 2 + core
     other_core = x_lo * 2 + 1 - core
 
-    own = rows.at[col // 2, pl.ds(pl.multiple_of(h * SHARD, SHARD), SHARD)]
-    load_rows = pltpu.make_async_copy(rows_hbm, own, load_sem.at[0])
-    load_rows.start()
+    def shard(fast, source):
+        lines = pl.ds(pl.multiple_of(source % 2 * SHARD, SHARD), SHARD)
+        return rows.at[fast, source // 2, lines]
+
+    load_rows = [
+        pltpu.make_async_copy(
+            rows_hbm.at[:, pl.ds(fast * HALF, HALF)], shard(fast, col), load_sem.at[fast]
+        )
+        for fast in (0, 1)
+    ]
+    for load in load_rows:
+        load.start()
 
     barrier = pltpu.get_barrier_semaphore()
 
@@ -57,7 +64,7 @@
     pl.semaphore_signal(barrier, inc=1, device_id=(other_core, col), device_id_type=MESH)
 
     loads = [
-        pltpu.make_async_copy(source, target, load_sem.at[n + 1])
+        pltpu.make_async_copy(source, target, load_sem.at[n + 2])
         for n, (source, target) in enumerate(
             (
                 (dest_hbm, dest),
@@ -103,18 +110,15 @@
         copy.wait()
 
     def place(unit):
-        q, fast, first, second, dh = unit
+        fast, first, second, dh = unit
         return peer(first, second, dh) if fast == 0 else peer(second, first, dh)
 
     def unit_view(unit, half):
-        source = place(unit)
-        width = HALF if half is None else HALF // 2
-        start = unit[1] * HALF + (half or 0) * width
-        lines = pl.ds(pl.multiple_of(source % 2 * SHARD + unit[0] * UNIT, UNIT), UNIT)
-        return rows.at[source // 2, lines, pl.ds(start, width)]
+        view = shard(unit[0], place(unit))
+        return view if half is None else view.at[pl.ds(half * SHARD // 2, SHARD // 2)]
 
     def unit_sem(unit, half):
-        q, fast, first, second, dh = unit
+        fast, first, second, dh = unit
         if second == 2 or (first == 2 and second and half != (0 if second < 0 else 1)):
             return stay_recv.at[0]
         kind = [
@@ -122,7 +126,7 @@
             (2, 0, 0), (2, 0, 1), (2, -1, 0), (2, 1, 1),
             (-1, -1, None), (-1, 1, None), (1, -1, None), (1, 1, None),
         ].index((first, second, half))
-        return unit_recv.at[((q * 2 + dh) * 2 + fast) * 12 + kind]
+        return unit_recv.at[(dh * 2 + fast) * 12 + kind]
 
     def unit_copy(unit, half, arrives, to):
         view = unit_view(unit, half)
@@ -139,13 +143,13 @@
         unit_copy(unit, half, unit, col).wait_recv()
 
     def send(unit, axis, step, half=None):
-        q, fast, first, second, dh = unit
+        fast, first, second, dh = unit
         if axis == fast:
             first = (first - step + 1) % 4 - 1
         else:
             second = (second - step + 1) % 4 - 1
         to = peer(step, 0, 0) if axis == 0 else peer(0, step, 0)
-        unit_copy(unit, half, (q, fast, first, second, dh), to).start()
+        unit_copy(unit, half, (fast, first, second, dh), to).start()
 
     def both_ways(unit, axis, half=None):
         send(unit, axis, 1, half)
@@ -154,58 +158,56 @@
     def forward(unit, axis, came):
         send(unit, axis, -came, 0 if came < 0 else 1)
 
-    def pair_copy(q, source):
-        lines = pl.ds(pl.multiple_of(source % 2 * SHARD + q * UNIT, UNIT), UNIT)
-        view = rows.at[source // 2, lines]
+    def pair_copy(fast, source):
         return pltpu.make_async_remote_copy(
-            src_ref=view,
-            dst_ref=view,
+            src_ref=shard(fast, source),
+            dst_ref=shard(fast, source),
             send_sem=pair_send.at[0],
-            recv_sem=pair_recv.at[q],
+            recv_sem=pair_recv.at[fast],
             device_id=(row, peer(0, 0, 1)),
             device_id_type=MESH,
         )
 
-    def stage0(q, dh):
-        if dh:
-            pair_copy(q, peer(0, 0, 1)).wait_recv()
+    def stage0(dh):
         for fast in (0, 1):
-            both_ways((q, fast, 0, 0, dh), fast)
+            if dh:
+                pair_copy(fast, peer(0, 0, 1)).wait_recv()
+            both_ways((fast, 0, 0, dh), fast)
         for fast in (0, 1):
-            both_ways((q, fast, 0, 0, dh), 1 - fast)
-
-    def stage1(q, dh):
+            both_ways((fast, 0, 0, dh), 1 - fast)
+
+    def stage1(dh):
         for came in (-1, 1):
             for fast in (0, 1):
-                unit = (q, fast, came, 0, dh)
+                unit = (fast, came, 0, dh)
                 arrived(unit)
                 forward(unit, fast, came)
                 both_ways(unit, 1 - fast)
 
-    def stage2(q, dh):
+    def stage2(dh):
         for came in (-1, 1):
             for fast in (0, 1):
-                unit = (q, fast, 0, came, dh)
+                unit = (fast, 0, came, dh)
                 arrived(unit)
                 forward(unit, 1 - fast, came)
         for half in (0, 1):
             for fast in (0, 1):
-                unit = (q, fast, 2, 0, dh)
+                unit = (fast, 2, 0, dh)
                 arrived(unit, half)
                 both_ways(unit, 1 - fast, half)
 
-    def stage3(q, dh):
+    def stage3(dh):
         for first in (-1, 1):
             for came in (-1, 1):
                 for fast in (0, 1):
-                    unit = (q, fast, first, came, dh)
+                    unit = (fast, first, came, dh)
                     arrived(unit)
                     forward(unit, 1 - fast, came)
 
-    def stage4(q, dh):
+    def stage4(dh):
         for came in (-1, 1):
             for fast in (0, 1):
-                unit = (q, fast, 2, came, dh)
+                unit = (fast, 2, came, dh)
                 arrived(unit, 0 if came < 0 else 1)
                 forward(unit, 1 - fast, came)
 
@@ -229,11 +231,11 @@
         panel_copy(part, beside, 0, beside).wait_recv()
         panel_copy(part, beside, 2, other_core).start()
 
-    load_rows.wait()
-    for q in range(PARTS):
-        pair_copy(q, col).start()
-    for q in range(PARTS):
-        stage0(q, 0)
+    for load in load_rows:
+        load.wait()
+    for fast in (0, 1):
+        pair_copy(fast, col).start()
+    stage0(0)
 
     for load in loads:
         load.wait()
@@ -252,20 +254,20 @@
     lax.fori_loop(0, CB, masked, 0)
     for part in range(PANEL_PARTS):
         panel_copy(part, row, 1, other_core).start()
-    stage1(0, 0)
-    stage0(0, 1)
+    stage1(0)
+    stage0(1)
     start_panels()
-    stage1(0, 1)
-    stage2(0, 0)
-    stage2(0, 1)
-    stage3(0, 0)
-    stage4(0, 0)
-    stage3(0, 1)
+    stage1(1)
+    stage2(0)
+    stage2(1)
+    stage3(0)
+    stage4(0)
+    stage3(1)
     for part in range(PANEL_PARTS - 1):
         pass_panel(part)
-    stage4(0, 1)
+    stage4(1)
     pass_panel(PANEL_PARTS - 1)
-    await_bytes(rows.at[pl.ds(0, 5)], stay_recv.at[0])
+    await_bytes(rows.at[0, pl.ds(0, 10)], stay_recv.at[0])
     await_bytes(panels.at[0], panel_recv.at[PANEL_PARTS])
     await_bytes(panels.at[0], panel_recv.at[PANEL_PARTS + 1])
     await_bytes(tile, tile_sem.at[0])
@@ -277,7 +279,7 @@
         cube = jnp.zeros((BS, BS), jnp.float32)
         for k in range(4):
             cube = cube + jnp.dot(
-                rows[i, :, k * PB * BS : (k + 1) * PB * BS],
+                rows[k // 2, i, :, k % 2 * PB * BS : (k % 2 + 1) * PB * BS],
                 panels[owners_ref[k], j],
                 preferred_element_type=jnp.float32,
             )
@@ -319,8 +321,8 @@
     keep = pltpu.make_async_copy(staged.at[0], mine, tile_sem.at[0])
     keep.start()
 
-    await_bytes(rows.at[pl.ds(0, RB - 1)], ring_send.at[0])
-    await_bytes(own, pair_send.at[0])
+    await_bytes(rows.at[:, pl.ds(0, RB - 1)], ring_send.at[0])
+    await_bytes(rows.at[0, 0], pair_send.at[0])
     for kind in range(3):
         await_bytes(panels.at[0], panel_send.at[kind])
     keep.wait()
@@ -337,7 +339,7 @@
         in_specs=[pl.BlockSpec(memory_space=pltpu.HBM)] * 8,
         out_specs=pl.BlockSpec(memory_space=pl.ANY),
         scratch_shapes=[
-            pltpu.VMEM((RB, BS, DEPTH), jnp.bfloat16),
+            pltpu.VMEM((2, RB, BS, HALF), jnp.bfloat16),
             pltpu.VMEM((4, CB, PB * BS, BS), jnp.bfloat16),
             pltpu.VMEM((PB * BS, CB * BS), jnp.bfloat16),
             pltpu.VMEM((CB, RB, BS, BS), jnp.bfloat16),
@@ -349,12 +351,12 @@
             pltpu.SMEM(owners.shape, jnp.int32),
             pltpu.SMEM(panel_mask.shape, jnp.int32),
             pltpu.SMEM((8, BS), jnp.int32),
-            sem((7,)),
-            sem((1,)),
-            sem((1,)),
-            sem((1,)),
-            sem((PARTS,)),
-            sem((PARTS * 48,)),
+            sem((8,)),
+            sem((1,)),
+            sem((1,)),
+            sem((1,)),
+            sem((2,)),
+            sem((48,)),
             sem((1,)),
             sem((3,)),
             sem((PANEL_PARTS + 2,)),

time: 84.6 us -> 84.6 us (level)
  no operation moved by 1% of the time
where the time goes in v4:
time: 84.6 us; the launch traced here: 84 us
  Pallas kernels  80.2 us (95%)
  local copies, waits for them, and re-layouts  3.16 us (4%)
    pallas_call x1, Pallas kernels, shards(): pl.pallas_call(kernel, out_shape=jax.ShapeDtypeStruct((NCOL * SLOTS, BS,...  80.2 us
    unnamed x1, local copies, waits for them, and re-layouts  3.16 us

profile of v4, /device:TPU:0, one launch (start us, length us, event | category | flops | bytes accessed | tf_op | source)
XLA Modules:
  0.0 84.0 jit_solution(3726145661321044631)
XLA Ops:
  0.7 80.2 %shard_map.82 = bf16[64,128,128]{2,1,0:T(8,128)(2,1)} custom-call(s32[1,48]{1,0:T(1,128)} %bitcast.4, s32[1,48]{1,0:T(1,128)} %bitcast.5, s32[1]{0:T(128)S(6)} %copy.10.counts_hbm, s32[4]{0:T(128)} %owners_hbm.1, s32[1,4,11]{2,1,0:T(4,128)} %mask_hbm.1, bf16[64,2048]{1,0:T(8,128)(2,1)} %rows_hbm.1, bf16[1,512,1408]{2,1,0:T(8,128)(2,1)} %panel_hbm.1, ...), custom_call_target="tpu_custom_call" | custom-call | flops 4300000256 | bytes 12000000 | tf_op jit(solution)/shard_map/pallas_call | solution.py:336
  80.8 3.2 %copy.11 = bf16[64,128,128]{2,1,0:T(8,128)(2,1)} copy(bf16[64,128,128]{2,1,0:T(8,128)(2,1)} %shard_map.82) | data formatting | bytes 4194304

commit v5 on v4

--- a/solution.py
+++ b/solution.py
@@ -101,7 +101,7 @@
         hit = slot == lax.broadcasted_iota(jnp.int32, (count, table.shape[1]), 1)
         block_row = (listed * 745) >> 13
         entry = lax.broadcasted_iota(jnp.int32, (count, 1), 0)
-        live = (entry < counts_ref[0]).astype(jnp.int32)
+        live = (entry < counts_ref[0, 0]).astype(jnp.int32)
         table[...] = jnp.zeros_like(table)
         for n, column in enumerate((block_row, listed - block_row * CB, live)):
             table[n : n + 1] = jnp.sum(jnp.where(hit, column, 0), axis=0, keepdims=True)
@@ -347,7 +347,7 @@
             pltpu.VMEM((1, count), jnp.int32),
             pltpu.VMEM((1, count), jnp.int32),
             pltpu.VMEM((8, BS), jnp.int32),
-            pltpu.SMEM(counts.shape, jnp.int32),
+            pltpu.SMEM((1, 1), jnp.int32),
             pltpu.SMEM(owners.shape, jnp.int32),
             pltpu.SMEM(panel_mask.shape, jnp.int32),
             pltpu.SMEM((8, BS), jnp.int32),
@@ -372,7 +372,7 @@
     )(
         block_ids.reshape(1, count),
         dest.reshape(1, count),
-        counts,
+        counts.reshape(1, 1),
         owners,
         panel_mask,
         x2_rows,

time: 84.6 us -> 84.6 us (level)
  no operation moved by 1% of the time
where the time goes in v5:
time: 84.6 us; the launch traced here: 84 us
  Pallas kernels  80.2 us (95%)
  local copies, waits for them, and re-layouts  3.16 us (4%)
    pallas_call x1, Pallas kernels, shards(): pl.pallas_call(kernel, out_shape=jax.ShapeDtypeStruct((NCOL * SLOTS, BS,...  80.2 us
    unnamed x1, local copies, waits for them, and re-layouts  3.16 us

profile of v5, /device:TPU:0, one launch (start us, length us, event | category | flops | bytes accessed | tf_op | source)
XLA Modules:
  0.0 84.0 jit_solution(3726145661321044631)
XLA Ops:
  0.7 80.2 %shard_map.82 = bf16[64,128,128]{2,1,0:T(8,128)(2,1)} custom-call(s32[1,48]{1,0:T(1,128)} %bitcast.6, s32[1,48]{1,0:T(1,128)} %bitcast.7, s32[1,1]{1,0:T(1,128)} %bitcast.4.counts_hbm, s32[4]{0:T(128)} %owners_hbm.1, s32[1,4,11]{2,1,0:T(4,128)} %mask_hbm.1, bf16[64,2048]{1,0:T(8,128)(2,1)} %rows_hbm.1, bf16[1,512,1408]{2,1,0:T(8,128)(2,1)} %panel_hbm.1, ...), custom_call_target="tpu_custom_call" | custom-call | flops 4300000256 | bytes 12000000 | tf_op jit(solution)/shard_map/pallas_call | solution.py:336
  80.8 3.2 %copy.11 = bf16[64,128,128]{2,1,0:T(8,128)(2,1)} copy(bf16[64,128,128]{2,1,0:T(8,128)(2,1)} %shard_map.82) | data formatting | bytes 4194304
